TPU v7x, 32 devices: a whole 2x2x4 slice. The times are simulated.
32 devices in a mesh: group: 2 (over y), src: 4 (over z), rcv: 4 (over x, core).
Axes of the slice: x: 2, y: 2, z: 4, core: 2. Of those that a mesh axis runs over, the one named last changes fastest.
Arguments:
- traces: bfloat16 [128, 36864], P(('group', 'src', 'rcv')), parts along dimension 0, may hold values from -6 to 6
- offsets: int32 [16], P('group'), parts along dimension 0, may hold values from 0 to 32768
- receiver_slots: int32 [8, 16], P(('group', 'rcv')), parts along dimension 0, may hold values from 0 to 15, each once within a row
Outputs:
- correlations: bfloat16 [128, 64, 128], P(('group', 'src'), 'rcv'), parts along dimension 0
There are 2 independent parts, one for each index of `group`. A program takes and returns all parts, laid end to end along the dimension named above; each array names one. Nothing has to cross between parts.
All inputs are finite; a program needn't handle non-finite values.
Results may differ from a plain program's by a relative error of at most 0.0065.
Values may be sent and summed in bfloat16 or wider, within the bound.
A program may use at most 64 MiB of HBM per device.

v0:
```python
import math

import jax
import jax.numpy as jnp
from jax import lax
from jax.sharding import PartitionSpec as P

SEG_LEN = 4096
NB = 512
LAGS = 128
LAG_STEP = 4
SEGS = 8


def dft_table():
    t_index = jnp.arange(SEG_LEN, dtype=jnp.int32)[:, None]
    k_index = jnp.arange(NB, dtype=jnp.int32)[None, :]
    phase = jnp.mod(t_index * k_index, SEG_LEN).astype(jnp.float32) * (2.0 * math.pi / SEG_LEN)
    return jnp.concatenate([jnp.cos(phase), -jnp.sin(phase)], axis=1).astype(jnp.bfloat16)


def lag_table():
    k_index = jnp.arange(NB, dtype=jnp.int32)[:, None]
    lag_shift = LAG_STEP * (jnp.arange(LAGS, dtype=jnp.int32)[None, :] - LAGS // 2)
    phase = jnp.mod(k_index * lag_shift, SEG_LEN).astype(jnp.float32) * (2.0 * math.pi / SEG_LEN)
    return jnp.concatenate([jnp.cos(phase), -jnp.sin(phase)], axis=0).astype(jnp.bfloat16)


def whiten(traces, offsets):
    table = dft_table()
    pieces = jax.vmap(lambda start: lax.dynamic_slice_in_dim(traces, start, SEG_LEN, 1))(offsets)
    pieces = jnp.transpose(pieces, (1, 0, 2)).reshape(-1, SEG_LEN)
    spectra = jnp.dot(pieces, table, preferred_element_type=jnp.float32)
    energy = jnp.mean(spectra * spectra, axis=-1, keepdims=True)
    white = (spectra / jnp.sqrt(energy + 1e-06)).astype(jnp.bfloat16)
    return white.reshape(traces.shape[0], SEGS, 2 * NB)


def four_sources(sources, receivers, lags):
    src_re = sources[..., :NB]
    src_im = sources[..., NB:]
    rec_re = receivers[..., :NB]
    rec_im = receivers[..., NB:]

    def pair(left, right):
        return jnp.einsum("sgk,rgk->srk", left, right, preferred_element_type=jnp.float32)

    real_part = pair(src_re, rec_re) + pair(src_im, rec_im)
    imag_part = pair(src_re, rec_im) - pair(src_im, rec_re)
    cross = jnp.concatenate([real_part, imag_part], axis=-1).astype(jnp.bfloat16)
    out = jnp.einsum("srk,kl->srl", cross, lags, preferred_element_type=jnp.float32)
    return (out * (1.0 / math.sqrt(SEGS * NB))).astype(jnp.bfloat16)


def correlate(sources, receivers, lags):
    src_count = sources.shape[0]
    grouped = sources.reshape(src_count // 4, 4, SEGS, 2 * NB)
    out = lax.map(lambda blk: four_sources(blk, receivers, lags), grouped)
    return out.reshape(src_count, receivers.shape[0], LAGS)


def on_device(traces, offsets, receiver_slots):
    white = whiten(traces, offsets)
    lags = lag_table()
    sources = lax.all_gather(white, "rcv", axis=0, tiled=True)
    block = correlate(sources, lax.all_gather(white, "src", axis=0, tiled=True), lags)
    return jnp.take(block, receiver_slots[0], axis=1)


def solution(mesh):
    in_specs = (P(("group", "src", "rcv"), None), P("group"), P(("group", "rcv"), None))
    out_specs = P(("group", "src"), "rcv", None)
    return jax.shard_map(
        on_device, mesh=mesh, in_specs=in_specs, out_specs=out_specs, check_vma=False
    )
```

profile of v0, /device:TPU:0, one launch (start us, length us, event | category | flops | bytes accessed | tf_op | source)
XLA Modules:
  0.0 121.1 jit_solution(13736536514290017647)
XLA Ops:
  0.0 0.7 fusion.40
  0.7 16.2 %while.12 = (s32[]{:T(128)}, bf16[4,36864]{1,0:T(4,128)(2,1)}, s32[8,2]{0,1:T(2,128)S(1)}, bf16[8,4,4096]{2,1,0:T(4,128)(2,1)S(1)}, s32[]{:T(128)}) while((s32[]{:T(128)}, bf16[4,36864]{1,0:T(4,128)(2,1)}, s32[8,2]{0,1:T(2,128)S(1)}, bf16[8,4,4096]{2,1,0:T(4,128)(2,1)S(1)}, s32[]{:T(128)}) %tuple.34), condition=%wide.while_cond, body=%wide.while_body.sunk | while | flops 2 | bytes 65633 | solution.py:31
  1.3 1.4 %bitcast_dynamic-update-slice_fusion.2 = bf16[8,4,4096]{2,1,0:T(4,128)(2,1)S(1)} fusion(bf16[8,4,4096]{2,1,0:T(4,128)(2,1)S(1)} %get-tuple-element.139, s32[]{:T(128)} %get-tuple-element.136, bf16[4,36864]{1,0:T(4,128)(2,1)} %get-tuple-element.142, s32[]{:T(128)} %bitcast.79), kind=kLoop, calls=%fused_computation.27.clone.1 | loop fusion | bytes 65544 | tf_op jit(solution)/shard_map/vmap()/gather
  3.3 1.4 %bitcast_dynamic-update-slice_fusion.2 = bf16[8,4,4096]{2,1,0:T(4,128)(2,1)S(1)} fusion(bf16[8,4,4096]{2,1,0:T(4,128)(2,1)S(1)} %get-tuple-element.139, s32[]{:T(128)} %get-tuple-element.136, bf16[4,36864]{1,0:T(4,128)(2,1)} %get-tuple-element.142, s32[]{:T(128)} %bitcast.79), kind=kLoop, calls=%fused_computation.27.clone.1 | loop fusion | bytes 65544 | tf_op jit(solution)/shard_map/vmap()/gather
  5.3 1.4 %bitcast_dynamic-update-slice_fusion.2 = bf16[8,4,4096]{2,1,0:T(4,128)(2,1)S(1)} fusion(bf16[8,4,4096]{2,1,0:T(4,128)(2,1)S(1)} %get-tuple-element.139, s32[]{:T(128)} %get-tuple-element.136, bf16[4,36864]{1,0:T(4,128)(2,1)} %get-tuple-element.142, s32[]{:T(128)} %bitcast.79), kind=kLoop, calls=%fused_computation.27.clone.1 | loop fusion | bytes 65544 | tf_op jit(solution)/shard_map/vmap()/gather
  7.3 1.4 %bitcast_dynamic-update-slice_fusion.2 = bf16[8,4,4096]{2,1,0:T(4,128)(2,1)S(1)} fusion(bf16[8,4,4096]{2,1,0:T(4,128)(2,1)S(1)} %get-tuple-element.139, s32[]{:T(128)} %get-tuple-element.136, bf16[4,36864]{1,0:T(4,128)(2,1)} %get-tuple-element.142, s32[]{:T(128)} %bitcast.79), kind=kLoop, calls=%fused_computation.27.clone.1 | loop fusion | bytes 65544 | tf_op jit(solution)/shard_map/vmap()/gather
  9.3 1.4 %bitcast_dynamic-update-slice_fusion.2 = bf16[8,4,4096]{2,1,0:T(4,128)(2,1)S(1)} fusion(bf16[8,4,4096]{2,1,0:T(4,128)(2,1)S(1)} %get-tuple-element.139, s32[]{:T(128)} %get-tuple-element.136, bf16[4,36864]{1,0:T(4,128)(2,1)} %get-tuple-element.142, s32[]{:T(128)} %bitcast.79), kind=kLoop, calls=%fused_computation.27.clone.1 | loop fusion | bytes 65544 | tf_op jit(solution)/shard_map/vmap()/gather
  11.4 1.4 %bitcast_dynamic-update-slice_fusion.2 = bf16[8,4,4096]{2,1,0:T(4,128)(2,1)S(1)} fusion(bf16[8,4,4096]{2,1,0:T(4,128)(2,1)S(1)} %get-tuple-element.139, s32[]{:T(128)} %get-tuple-element.136, bf16[4,36864]{1,0:T(4,128)(2,1)} %get-tuple-element.142, s32[]{:T(128)} %bitcast.79), kind=kLoop, calls=%fused_computation.27.clone.1 | loop fusion | bytes 65544 | tf_op jit(solution)/shard_map/vmap()/gather
  13.4 1.4 %bitcast_dynamic-update-slice_fusion.2 = bf16[8,4,4096]{2,1,0:T(4,128)(2,1)S(1)} fusion(bf16[8,4,4096]{2,1,0:T(4,128)(2,1)S(1)} %get-tuple-element.139, s32[]{:T(128)} %get-tuple-element.136, bf16[4,36864]{1,0:T(4,128)(2,1)} %get-tuple-element.142, s32[]{:T(128)} %bitcast.79), kind=kLoop, calls=%fused_computation.27.clone.1 | loop fusion | bytes 65544 | tf_op jit(solution)/shard_map/vmap()/gather
  15.4 1.4 %bitcast_dynamic-update-slice_fusion.2 = bf16[8,4,4096]{2,1,0:T(4,128)(2,1)S(1)} fusion(bf16[8,4,4096]{2,1,0:T(4,128)(2,1)S(1)} %get-tuple-element.139, s32[]{:T(128)} %get-tuple-element.136, bf16[4,36864]{1,0:T(4,128)(2,1)} %get-tuple-element.142, s32[]{:T(128)} %bitcast.79), kind=kLoop, calls=%fused_computation.27.clone.1 | loop fusion | bytes 65544 | tf_op jit(solution)/shard_map/vmap()/gather
  16.8 33.9 %negate_convert_fusion = (bf16[4096,512]{1,0:T(8,128)(2,1)S(1)}, bf16[4096,512]{1,0:T(8,128)(2,1)S(1)}) fusion(), kind=kLoop, calls=%fused_computation.39 | loop fusion | flops 35651584 | bytes 8388608 | tf_op jit(solution)/shard_map/convert.7
  50.8 1.6 %multiply_reduce_fusion = (f32[32]{0:T(128)S(1)}, f32[32,1024]{1,0:T(8,128)S(1)}) fusion(bf16[4096,512]{1,0:T(8,128)(2,1)S(1)} %get-tuple-element.73, bf16[4096,512]{1,0:T(8,128)(2,1)S(1)} %get-tuple-element.74, bf16[8,4,4096]{2,1,0:T(4,128)(2,1)S(1)} %get-tuple-element.40), kind=kOutput, calls=%fused_computation.59 | convolution fusion | flops 285278176 | bytes 8781952 | tf_op jit(solution)/shard_map/dot_general | solution.py:33
  52.5 15.6 %all_gather.7 = bf16[16,8,1024]{2,1,0:T(8,128)(2,1)S(1)} all-gather(bf16[4,8,1024]{2,1,0:T(8,128)(2,1)S(1)} %fusion.39), channel_id=1, replica_groups=mesh['group'=2,'src'=4,'rcv'=4] {'src'}, dimensions={0}, use_global_device_ids=true | all-gather | bytes 327680 | tf_op jit(solution)/shard_map/all_gather | solution.py:66
  68.2 1.6 %copy.17 = bf16[16,8,1024]{0,1,2:T(8,128)(2,1)S(1)} copy(bf16[16,8,1024]{2,1,0:T(8,128)(2,1)S(1)} %all_gather.7) | data formatting | bytes 524288 | tf_op jit(solution)/shard_map/while | solution.py:58
  69.8 6.2 %all_gather.6 = bf16[16,8,1024]{2,1,0:T(8,128)(2,1)} all-gather(bf16[4,8,1024]{2,1,0:T(8,128)(2,1)S(1)} %fusion.39), channel_id=1, replica_groups=mesh['group'=2,'src'=4,'rcv'=4] {'rcv'}, dimensions={0}, use_global_device_ids=true | all-gather | bytes 327680 | tf_op jit(solution)/shard_map/all_gather | solution.py:65
  76.0 1.1 cosine_convert_fusion.1
  77.2 0.7 pad_maximum_fusion
  77.9 41.0 %while.11 = (s32[]{:T(128)}, bf16[4,4,16,128]{3,1,0,2:T(4,128)(2,1)}, bf16[4,4,8,1024]{3,2,1,0:T(8,128)(2,1)}, bf16[16,8,1024]{0,1,2:T(8,128)(2,1)S(1)}, bf16[1024,128]{1,0:T(8,128)(2,1)}, /*index=5*/s32[]{:T(128)}) while((s32[]{:T(128)}, bf16[4,4,16,128]{3,1,0,2:T(4,128)(2,1)}, bf16[4,4,8,1024]{3,2,1,0:T(8,128)(2,1)}, ...), condition=%wide.region_2.3_spmd, body=%wide.region_1.2_spmd.sunk | while | flops 19283968 | bytes 4768385 | solution.py:58
  77.9 0.9 constant_dynamic-slice_fusion.4
  78.8 0.7 copy.35
  79.5 0.7 fusion.97
  80.3 1.5 %fusion.99 = bf16[4,16,512]{1,0,2:T(4,128)(2,1)} fusion(f32[512,4,16]{2,1,0:T(4,128)S(1)} %fusion.97, bf16[1,4,8,1024]{2,1,3,0:T(4,128)(2,1)S(1)} %copy.35, bf16[16,8,512]{0,1,2:T(8,128)(2,1)S(1)} %fusion.98), kind=kOutput, calls=%fused_computation.6.clone.2 | convolution fusion | flops 589824 | bytes 393216 | tf_op jit(solution)/shard_map/while/body/eval_jaxpr/sgk,rgk->srk/dot_general | solution.py:46
  81.8 1.9 %copy.37 = bf16[4,16,512]{2,1,0:T(8,128)(2,1)} copy(bf16[4,16,512]{1,0,2:T(4,128)(2,1)} %fusion.99) | data formatting | bytes 131072 | tf_op jit(solution)/shard_map/while/body/eval_jaxpr/add | solution.py:48
  83.8 0.7 fusion.93
  84.5 1.5 %fusion.95 = bf16[4,16,512]{1,0,2:T(4,128)(2,1)} fusion(f32[512,4,16]{2,1,0:T(4,128)S(1)} %fusion.93, bf16[1,4,8,1024]{2,1,3,0:T(4,128)(2,1)S(1)} %copy.35, bf16[16,8,512]{0,1,2:T(8,128)(2,1)S(1)} %fusion.94), kind=kOutput, calls=%fused_computation.5.clone.2 | convolution fusion | flops 589824 | bytes 393216 | tf_op jit(solution)/shard_map/while/body/eval_jaxpr/sgk,rgk->srk/dot_general | solution.py:46
  86.1 1.3 %copy.36 = bf16[4,16,512]{2,1,0:T(8,128)(2,1)S(1)} copy(bf16[4,16,512]{1,0,2:T(4,128)(2,1)} %fusion.95) | data formatting | bytes 131072 | tf_op jit(solution)/shard_map/while/body/eval_jaxpr/sub | solution.py:49
  88.2 0.8 constant_dynamic-slice_fusion.4
  89.8 0.7 fusion.97
  90.5 1.5 %fusion.99 = bf16[4,16,512]{1,0,2:T(4,128)(2,1)} fusion(f32[512,4,16]{2,1,0:T(4,128)S(1)} %fusion.97, bf16[1,4,8,1024]{2,1,3,0:T(4,128)(2,1)S(1)} %copy.35, bf16[16,8,512]{0,1,2:T(8,128)(2,1)S(1)} %fusion.98), kind=kOutput, calls=%fused_computation.6.clone.2 | convolution fusion | flops 589824 | bytes 393216 | tf_op jit(solution)/shard_map/while/body/eval_jaxpr/sgk,rgk->srk/dot_general | solution.py:46
  92.0 1.9 %copy.37 = bf16[4,16,512]{2,1,0:T(8,128)(2,1)} copy(bf16[4,16,512]{1,0,2:T(4,128)(2,1)} %fusion.99) | data formatting | bytes 131072 | tf_op jit(solution)/shard_map/while/body/eval_jaxpr/add | solution.py:48
  94.0 0.7 fusion.93
  94.8 1.5 %fusion.95 = bf16[4,16,512]{1,0,2:T(4,128)(2,1)} fusion(f32[512,4,16]{2,1,0:T(4,128)S(1)} %fusion.93, bf16[1,4,8,1024]{2,1,3,0:T(4,128)(2,1)S(1)} %copy.35, bf16[16,8,512]{0,1,2:T(8,128)(2,1)S(1)} %fusion.94), kind=kOutput, calls=%fused_computation.5.clone.2 | convolution fusion | flops 589824 | bytes 393216 | tf_op jit(solution)/shard_map/while/body/eval_jaxpr/sgk,rgk->srk/dot_general | solution.py:46
  96.3 1.3 %copy.36 = bf16[4,16,512]{2,1,0:T(8,128)(2,1)S(1)} copy(bf16[4,16,512]{1,0,2:T(4,128)(2,1)} %fusion.95) | data formatting | bytes 131072 | tf_op jit(solution)/shard_map/while/body/eval_jaxpr/sub | solution.py:49
  98.4 0.8 constant_dynamic-slice_fusion.4
  100.0 0.7 fusion.97
  100.8 1.5 %fusion.99 = bf16[4,16,512]{1,0,2:T(4,128)(2,1)} fusion(f32[512,4,16]{2,1,0:T(4,128)S(1)} %fusion.97, bf16[1,4,8,1024]{2,1,3,0:T(4,128)(2,1)S(1)} %copy.35, bf16[16,8,512]{0,1,2:T(8,128)(2,1)S(1)} %fusion.98), kind=kOutput, calls=%fused_computation.6.clone.2 | convolution fusion | flops 589824 | bytes 393216 | tf_op jit(solution)/shard_map/while/body/eval_jaxpr/sgk,rgk->srk/dot_general | solution.py:46
  102.3 1.9 %copy.37 = bf16[4,16,512]{2,1,0:T(8,128)(2,1)} copy(bf16[4,16,512]{1,0,2:T(4,128)(2,1)} %fusion.99) | data formatting | bytes 131072 | tf_op jit(solution)/shard_map/while/body/eval_jaxpr/add | solution.py:48
  104.3 0.7 fusion.93
  105.1 1.5 %fusion.95 = bf16[4,16,512]{1,0,2:T(4,128)(2,1)} fusion(f32[512,4,16]{2,1,0:T(4,128)S(1)} %fusion.93, bf16[1,4,8,1024]{2,1,3,0:T(4,128)(2,1)S(1)} %copy.35, bf16[16,8,512]{0,1,2:T(8,128)(2,1)S(1)} %fusion.94), kind=kOutput, calls=%fused_computation.5.clone.2 | convolution fusion | flops 589824 | bytes 393216 | tf_op jit(solution)/shard_map/while/body/eval_jaxpr/sgk,rgk->srk/dot_general | solution.py:46
  106.6 1.3 %copy.36 = bf16[4,16,512]{2,1,0:T(8,128)(2,1)S(1)} copy(bf16[4,16,512]{1,0,2:T(4,128)(2,1)} %fusion.95) | data formatting | bytes 131072 | tf_op jit(solution)/shard_map/while/body/eval_jaxpr/sub | solution.py:49
  108.7 0.8 constant_dynamic-slice_fusion.4
  110.3 0.7 fusion.97
  111.0 1.5 %fusion.99 = bf16[4,16,512]{1,0,2:T(4,128)(2,1)} fusion(f32[512,4,16]{2,1,0:T(4,128)S(1)} %fusion.97, bf16[1,4,8,1024]{2,1,3,0:T(4,128)(2,1)S(1)} %copy.35, bf16[16,8,512]{0,1,2:T(8,128)(2,1)S(1)} %fusion.98), kind=kOutput, calls=%fused_computation.6.clone.2 | convolution fusion | flops 589824 | bytes 393216 | tf_op jit(solution)/shard_map/while/body/eval_jaxpr/sgk,rgk->srk/dot_general | solution.py:46
  112.6 1.9 %copy.37 = bf16[4,16,512]{2,1,0:T(8,128)(2,1)} copy(bf16[4,16,512]{1,0,2:T(4,128)(2,1)} %fusion.99) | data formatting | bytes 131072 | tf_op jit(solution)/shard_map/while/body/eval_jaxpr/add | solution.py:48
  114.5 0.7 fusion.93
  115.3 1.5 %fusion.95 = bf16[4,16,512]{1,0,2:T(4,128)(2,1)} fusion(f32[512,4,16]{2,1,0:T(4,128)S(1)} %fusion.93, bf16[1,4,8,1024]{2,1,3,0:T(4,128)(2,1)S(1)} %copy.35, bf16[16,8,512]{0,1,2:T(8,128)(2,1)S(1)} %fusion.94), kind=kOutput, calls=%fused_computation.5.clone.2 | convolution fusion | flops 589824 | bytes 393216 | tf_op jit(solution)/shard_map/while/body/eval_jaxpr/sgk,rgk->srk/dot_general | solution.py:46
  116.8 1.3 %copy.36 = bf16[4,16,512]{2,1,0:T(8,128)(2,1)S(1)} copy(bf16[4,16,512]{1,0,2:T(4,128)(2,1)} %fusion.95) | data formatting | bytes 131072 | tf_op jit(solution)/shard_map/while/body/eval_jaxpr/sub | solution.py:49
  119.0 1.4 %gather_fusion = bf16[16,16,128]{2,1,0:T(8,128)(2,1)S(1)} fusion(bf16[16,16,128]{2,0,1:T(8,128)(2,1)} %bitcast.80, s32[1024]{0:T(1024)S(1)} %pad_clamp_fusion), kind=kCustom, calls=%fused_computation | custom fusion | bytes 131136 | tf_op jit(solution)/shard_map/jit(_take)/gather | solution.py:67
  (72 shorter events, 11.9 us)
Async XLA Ops:
  77.9 41.0 %copy-start.2 = (s32[1,16]{1,0:T(1,128)S(1)}, s32[1,16]{1,0:T(1,128)}, u32[]{:S(2)}) copy-start(s32[1,16]{1,0:T(1,128)} %param.7) | copy-start | bytes 196
  84.5 2.8 %copy-start = (bf16[1024,128]{1,0:T(8,128)(2,1)S(1)}, bf16[1024,128]{1,0:T(8,128)(2,1)}, u32[]{:S(2)}) copy-start(bf16[1024,128]{1,0:T(8,128)(2,1)} %get-tuple-element.162) | copy-start | bytes 786436 | tf_op jit(solution)/shard_map/while
  84.5 2.8 %copy-start.1 = (bf16[4,16,512]{2,1,0:T(8,128)(2,1)S(1)}, bf16[4,16,512]{2,1,0:T(8,128)(2,1)}, u32[]{:S(2)}) copy-start(bf16[4,16,512]{2,1,0:T(8,128)(2,1)} %copy.37) | copy-start | bytes 196612 | tf_op jit(solution)/shard_map/while
  94.8 2.8 %copy-start = (bf16[1024,128]{1,0:T(8,128)(2,1)S(1)}, bf16[1024,128]{1,0:T(8,128)(2,1)}, u32[]{:S(2)}) copy-start(bf16[1024,128]{1,0:T(8,128)(2,1)} %get-tuple-element.162) | copy-start | bytes 786436 | tf_op jit(solution)/shard_map/while
  94.8 2.8 %copy-start.1 = (bf16[4,16,512]{2,1,0:T(8,128)(2,1)S(1)}, bf16[4,16,512]{2,1,0:T(8,128)(2,1)}, u32[]{:S(2)}) copy-start(bf16[4,16,512]{2,1,0:T(8,128)(2,1)} %copy.37) | copy-start | bytes 196612 | tf_op jit(solution)/shard_map/while
  105.0 2.8 %copy-start = (bf16[1024,128]{1,0:T(8,128)(2,1)S(1)}, bf16[1024,128]{1,0:T(8,128)(2,1)}, u32[]{:S(2)}) copy-start(bf16[1024,128]{1,0:T(8,128)(2,1)} %get-tuple-element.162) | copy-start | bytes 786436 | tf_op jit(solution)/shard_map/while
  105.0 2.8 %copy-start.1 = (bf16[4,16,512]{2,1,0:T(8,128)(2,1)S(1)}, bf16[4,16,512]{2,1,0:T(8,128)(2,1)}, u32[]{:S(2)}) copy-start(bf16[4,16,512]{2,1,0:T(8,128)(2,1)} %copy.37) | copy-start | bytes 196612 | tf_op jit(solution)/shard_map/while
  115.3 2.8 %copy-start = (bf16[1024,128]{1,0:T(8,128)(2,1)S(1)}, bf16[1024,128]{1,0:T(8,128)(2,1)}, u32[]{:S(2)}) copy-start(bf16[1024,128]{1,0:T(8,128)(2,1)} %get-tuple-element.162) | copy-start | bytes 786436 | tf_op jit(solution)/shard_map/while
  115.3 2.8 %copy-start.1 = (bf16[4,16,512]{2,1,0:T(8,128)(2,1)S(1)}, bf16[4,16,512]{2,1,0:T(8,128)(2,1)}, u32[]{:S(2)}) copy-start(bf16[4,16,512]{2,1,0:T(8,128)(2,1)} %copy.37) | copy-start | bytes 196612 | tf_op jit(solution)/shard_map/while
where the time goes:
time: 122 us; the launch traced here: 121 us
  local copies, waits for them, and re-layouts  42.1 us (35%)
  other arithmetic  36.6 us (30%)
  blocking collectives  21.9 us (18%)
  matrix products  20 us (16%)
    another operation x2, other arithmetic  35 us
    dot_general x16, matrix products, pair(): jnp.einsum('sgk,rgk->srk', left, right, preferred_element_type=jnp.float32)  17.6 us
    gather x24, local copies, waits for them, and re-layouts  16 us
    all_gather x1, blocking collectives, on_device(): lax.all_gather(white, 'src', axis=0, tiled=True)  15.6 us
    add x4, local copies, waits for them, and re-layouts, four_sources(): real_part = pair(src_re, rec_re) + pair(src_im, rec_im)  7.62 us
    all_gather x1, blocking collectives, on_device(): sources = lax.all_gather(white, 'rcv', axis=0, tiled=True)  6.24 us
    dynamic_slice x8, local copies, waits for them, and re-layouts, correlate(): out = lax.map(lambda blk: four_sources(blk, receivers, lags), grouped)  6.01 us
    sub x4, local copies, waits for them, and re-layouts, four_sources(): imag_part = pair(src_re, rec_im) - pair(src_im, rec_re)  5.05 us

commit v1 on v0

v1 whole, which is shorter than its diff:
```python
import functools
import math

import jax
import jax.numpy as jnp
import numpy as np
from jax import lax
from jax.experimental import pallas as pl
from jax.experimental.pallas import tpu as pltpu
from jax.sharding import PartitionSpec as P

SEG_LEN = 4096
NB = 512
LAGS = 128
LAG_STEP = 4
RADIX = 4
FOLD = SEG_LEN // RADIX
BINS = NB // RADIX
MESH = pl.DeviceIdType.MESH


def tables():
    k = RADIX * np.arange(BINS)[None, :] + np.arange(RADIX)[:, None]
    t = np.arange(FOLD)[:, None, None]
    dft = 2.0 * math.pi / SEG_LEN * ((t * k[None]) % SEG_LEN)
    dft = np.stack([np.cos(dft), -np.sin(dft)], axis=2).reshape(FOLD, 2 * NB)
    tau = LAG_STEP * (np.arange(LAGS) - LAGS // 2)
    lag = 2.0 * math.pi / SEG_LEN * ((k[:, :, None] * tau) % SEG_LEN)
    lag = np.stack([np.cos(lag), -np.sin(lag)], axis=1).reshape(2 * NB, LAGS)
    return dft.astype(np.float32).astype(jnp.bfloat16), lag.astype(np.float32).astype(jnp.bfloat16)


def dot(left, right):
    return jnp.dot(left, right, preferred_element_type=jnp.float32)


def fold(segs, ch, offsets, traces, out, folded):
    window = traces.shape[1]
    lane = lax.broadcasted_iota(jnp.int32, (ch, 128), 1)
    for g in range(segs):
        start = offsets[g]
        shift = lax.rem(start, 128)
        base = pl.multiple_of(start - shift, 128)
        last = pl.multiple_of(jnp.minimum(base + SEG_LEN, window - 128), 128)
        main = traces[:, pl.ds(base, SEG_LEN)].astype(jnp.float32)
        extra = traces[:, pl.ds(last, 128)].astype(jnp.float32)
        back = lax.rem(128 - shift, 128)
        turned = [pltpu.roll(main[:, j * 128:(j + 1) * 128], back, 1) for j in range(SEG_LEN // 128)]
        turned.append(pltpu.roll(extra, back, 1))
        keep = lane < 128 - shift
        piece = [jnp.where(keep, turned[j], turned[j + 1]) for j in range(SEG_LEN // 128)]
        step = FOLD // 128
        here = slice(g * ch, (g + 1) * ch)
        for j in range(step):
            x0, x1, x2, x3 = (piece[q * step + j] for q in range(RADIX))
            even, odd = x0 + x2, x1 + x3
            at = slice(j * 128, (j + 1) * 128)
            folded[0, here, at] = even + odd
            folded[1, here, at] = even - odd
            folded[2, here, at] = x0 - x2
            folded[3, here, at] = x1 - x3
    out[...] = folded[...].astype(jnp.bfloat16)


def body(
    n_src, n_rcv, segs, ch,
    folded, dft, lag, corr,
    row_slots, col_slots, sources, receivers,
    row_send, row_recv, col_send, col_recv,
):
    me_r = lax.axis_index("rcv")
    me_s = lax.axis_index("src")
    rows = segs * ch

    barrier = pltpu.get_barrier_semaphore()
    for d in range(1, n_rcv):
        pl.semaphore_signal(barrier, inc=1, device_id={"rcv": lax.rem(me_r + d, n_rcv)}, device_id_type=MESH)

    def greet(d, _):
        pl.semaphore_signal(barrier, inc=1, device_id={"src": lax.rem(me_s + d, n_src)}, device_id_type=MESH)
        return 0

    lax.fori_loop(1, n_src, greet, 0)

    width = 2 * BINS
    p0 = dot(folded[0], dft[:, 0:width])
    p2 = dot(folded[1], dft[:, 2 * width:3 * width])
    both = folded[2:4].reshape(2 * rows, FOLD)
    p1 = dot(both, dft[:, width:2 * width])
    p3 = dot(both, dft[:, 3 * width:4 * width])
    parts = [
        p0[:, :BINS], p0[:, BINS:],
        p1[:rows, :BINS] + p1[rows:, BINS:], p1[:rows, BINS:] - p1[rows:, :BINS],
        p2[:, :BINS], p2[:, BINS:],
        p3[:rows, :BINS] - p3[rows:, BINS:], p3[:rows, BINS:] + p3[rows:, :BINS],
    ]
    spectra = jnp.concatenate(parts, axis=1)
    energy = jnp.sum(spectra * spectra, axis=1, keepdims=True) * (1.0 / (2 * NB))
    white = (spectra * (1.0 / jnp.sqrt(energy + 1e-06))).astype(jnp.bfloat16)
    row_slots[me_r] = white
    col_slots[me_s] = white

    pl.semaphore_wait(barrier, n_rcv - 1 + n_src - 1)

    def row_copy(to, slot):
        return pltpu.make_async_remote_copy(
            src_ref=row_slots.at[slot], dst_ref=row_slots.at[slot],
            send_sem=row_send.at[to], recv_sem=row_recv.at[slot],
            device_id={"rcv": to}, device_id_type=MESH,
        )

    def col_copy(to, slot):
        return pltpu.make_async_remote_copy(
            src_ref=col_slots.at[slot], dst_ref=col_slots.at[slot],
            send_sem=col_send.at[to], recv_sem=col_recv.at[slot],
            device_id={"src": to}, device_id_type=MESH,
        )

    for d in range(1, n_rcv):
        row_copy(lax.rem(me_r + d, n_rcv), me_r).start()

    def send(d, _):
        col_copy(lax.rem(me_s + d, n_src), me_s).start()
        return 0

    lax.fori_loop(1, n_src, send, 0)

    for d in range(1, n_rcv):
        other = lax.rem(me_r + d, n_rcv)
        row_copy(other, other).wait_recv()
    for j in range(n_rcv):
        block = row_slots[j].astype(jnp.float32)
        for g in range(segs):
            sources[g, j * ch:(j + 1) * ch, :] = block[g * ch:(g + 1) * ch]

    n_here = n_rcv * ch

    def shard(p):
        receivers[...] = col_slots[p].astype(jnp.float32)
        cross = []
        for r in range(RADIX):
            at_re = slice(r * width, r * width + BINS)
            at_im = slice(r * width + BINS, (r + 1) * width)
            re = im = 0.0
            for g in range(segs):
                s_re = sources[g, :, at_re][None]
                s_im = sources[g, :, at_im][None]
                r_re = receivers[g * ch:(g + 1) * ch, at_re][:, None]
                r_im = receivers[g * ch:(g + 1) * ch, at_im][:, None]
                re = re + (s_re * r_re + s_im * r_im)
                im = im + (s_re * r_im - s_im * r_re)
            cross += [re.astype(jnp.bfloat16).reshape(ch * n_here, BINS), im.astype(jnp.bfloat16).reshape(ch * n_here, BINS)]
        done = dot(jnp.concatenate(cross, axis=1), lag[...]) * (1.0 / math.sqrt(segs * NB))
        corr[pl.ds(p * ch, ch)] = done.reshape(ch, n_here, LAGS)

    shard(me_s)

    def arrive(d, _):
        other = lax.rem(me_s + d, n_src)
        col_copy(other, other).wait_recv()
        shard(other)
        return 0

    lax.fori_loop(1, n_src, arrive, 0)

    for d in range(1, n_rcv):
        row_copy(lax.rem(me_r + d, n_rcv), me_r).wait_send()

    def sent(d, _):
        col_copy(lax.rem(me_s + d, n_src), me_s).wait_send()
        return 0

    lax.fori_loop(1, n_src, sent, 0)


def arrange(slots, corr, out, placed):
    n_cols, n_here = corr.shape[:2]

    def place(q, _):
        tile = corr[slots[0, q]]
        for s in range(n_here):
            placed[s, pl.ds(q, 1), :] = tile[s:s + 1]
        return 0

    lax.fori_loop(0, n_cols, place, 0)
    out[...] = placed[...].astype(jnp.bfloat16)


def on_device(n_src, n_rcv, traces, offsets, receiver_slots):
    dft, lag = tables()
    ch = traces.shape[0]
    segs = offsets.shape[0]
    rows = segs * ch
    n_here, n_cols = n_rcv * ch, n_src * ch
    vmem = pl.BlockSpec(memory_space=pltpu.VMEM)
    smem = pl.BlockSpec(memory_space=pltpu.SMEM)
    room = 40 * 1024 * 1024
    folded = pl.pallas_call(
        functools.partial(fold, segs, ch),
        out_shape=jax.ShapeDtypeStruct((RADIX, rows, FOLD), jnp.bfloat16),
        in_specs=[smem, vmem],
        out_specs=vmem,
        scratch_shapes=[pltpu.VMEM((RADIX, rows, FOLD), jnp.float32)],
        compiler_params=pltpu.CompilerParams(vmem_limit_bytes=room),
    )(offsets, traces)
    corr = pl.pallas_call(
        functools.partial(body, n_src, n_rcv, segs, ch),
        out_shape=jax.ShapeDtypeStruct((n_cols, n_here, LAGS), jnp.float32),
        in_specs=[vmem] * 3,
        out_specs=vmem,
        scratch_shapes=[
            pltpu.VMEM((n_rcv, rows, 2 * NB), jnp.bfloat16),
            pltpu.VMEM((n_src, rows, 2 * NB), jnp.bfloat16),
            pltpu.VMEM((segs, n_here, 2 * NB), jnp.float32),
            pltpu.VMEM((rows, 2 * NB), jnp.float32),
            pltpu.SemaphoreType.DMA((n_rcv,)),
            pltpu.SemaphoreType.DMA((n_rcv,)),
            pltpu.SemaphoreType.DMA((n_src,)),
            pltpu.SemaphoreType.DMA((n_src,)),
        ],
        compiler_params=pltpu.CompilerParams(
            collective_id=0, has_side_effects=True, vmem_limit_bytes=room
        ),
    )(folded, jnp.asarray(dft), jnp.asarray(lag))
    return pl.pallas_call(
        arrange,
        out_shape=jax.ShapeDtypeStruct((n_here, n_cols, LAGS), jnp.bfloat16),
        in_specs=[smem, vmem],
        out_specs=vmem,
        scratch_shapes=[pltpu.VMEM((n_here, n_cols, LAGS), jnp.float32)],
        compiler_params=pltpu.CompilerParams(vmem_limit_bytes=room),
    )(receiver_slots, corr)


def solution(mesh):
    in_specs = (P(("group", "src", "rcv"), None), P("group"), P(("group", "rcv"), None))
    out_specs = P(("group", "src"), "rcv", None)
    return jax.shard_map(
        functools.partial(on_device, mesh.shape["src"], mesh.shape["rcv"]),
        mesh=mesh, in_specs=in_specs, out_specs=out_specs, check_vma=False,
    )
```

time: 122 us -> 19 us (0.16)
  local copies, waits for them, and re-layouts: 42.1 us -> 4.16 us
  other arithmetic: 36.6 us -> 0 us
  blocking collectives: 21.9 us -> 0 us
  matrix products: 20 us -> 0 us
  Pallas kernels: 0 us -> 14.6 us
    another operation x2 -> x0, other arithmetic: 35 us -> none
    all_gather x2 -> x0, blocking collectives: 21.9 us -> none  [the longest x1 15.6 us: on_device(): lax.all_gather(white, 'src', axis=0, tiled=True)]
    dot_general x21 -> x0, matrix products: 20 us -> none  [the longest x16 17.6 us: pair(): jnp.einsum('sgk,rgk->srk', left, right, preferred_element_type=jnp.float32)]
    gather x25 -> x0, local copies, waits for them, and re-layouts: 17.4 us -> none
    pallas_call x0 -> x3, Pallas kernels: none -> 14.6 us  [the longest x1 12.5 us: on_device(): pl.pallas_call(functools.partial(body, n_src, n_rcv, segs, ch), out_shape...]
    add x4 -> x0, local copies, waits for them, and re-layouts: 7.62 us -> none  [four_sources(): real_part = pair(src_re, rec_re) + pair(src_im, rec_im)]
    dynamic_slice x8 -> x0, local copies, waits for them, and re-layouts: 6.01 us -> none  [correlate(): out = lax.map(lambda blk: four_sources(blk, receivers, lags), grouped)]
    sub x4 -> x0, local copies, waits for them, and re-layouts: 5.05 us -> none  [four_sources(): imag_part = pair(src_re, rec_im) - pair(src_im, rec_re)]
where the time goes in v1:
time: 19 us; the launch traced here: 18.8 us
  Pallas kernels  14.6 us (77%)
  local copies, waits for them, and re-layouts  4.16 us (22%)
    pallas_call x1, Pallas kernels, on_device(): pl.pallas_call(functools.partial(body, n_src, n_rcv, segs, ch), out_shape...  12.5 us
    unnamed x10, local copies, waits for them, and re-layouts  4.16 us
    pallas_call x1, Pallas kernels, on_device(): pl.pallas_call(arrange, out_shape=jax.ShapeDtypeStruct((n_here, n_cols, L...  1.32 us
    pallas_call x1, Pallas kernels, on_device(): pl.pallas_call(functools.partial(fold, segs, ch), out_shape=jax.ShapeDtyp...  0.8 us

profile of v1, /device:TPU:0, one launch (start us, length us, event | category | flops | bytes accessed | tf_op | source)
XLA Modules:
  0.0 18.8 jit_solution(15946348229680467421)
XLA Ops:
  0.0 0.0 copy-start.1
  0.0 1.0 %copy-done.1 = bf16[4,36864]{1,0:T(4,128)(2,1)S(1)} copy-done((bf16[4,36864]{1,0:T(4,128)(2,1)S(1)}, bf16[4,36864]{1,0:T(4,128)(2,1)}, u32[]{:S(2)}) %copy-start.1) | copy-done | bytes 294936
  1.0 0.0 copy-start.3
  1.0 0.7 %copy-done.3 = s32[8]{0:T(128)S(1)} copy-done((s32[8]{0:T(128)S(1)}, s32[8]{0:T(128)}, u32[]{:S(2)}) %copy-start.3) | copy-done | bytes 56
  1.6 0.0 copy-start.4
  1.6 0.8 %shard_map.55.folded = bf16[4,32,1024]{2,1,0:T(8,128)(2,1)S(1)} custom-call(s32[8]{0:T(128)S(1)} %copy-done.3, bf16[4,36864]{1,0:T(4,128)(2,1)S(1)} %copy-done.1), custom_call_target="tpu_custom_call" | custom-call | tf_op jit(solution)/shard_map/pallas_call | solution.py:198
  2.4 0.0 copy-start
  2.4 1.6 %copy-done = bf16[1024,1024]{1,0:T(8,128)(2,1)S(1)} copy-done((bf16[1024,1024]{1,0:T(8,128)(2,1)S(1)}, bf16[1024,1024]{1,0:T(8,128)(2,1)}, u32[]{:S(2)}) %copy-start) | copy-done | bytes 2097176
  4.0 0.0 copy-start.2
  4.0 0.9 %copy-done.2 = bf16[1024,128]{1,0:T(8,128)(2,1)S(1)} copy-done((bf16[1024,128]{1,0:T(8,128)(2,1)S(1)}, bf16[1024,128]{1,0:T(8,128)(2,1)}, u32[]{:S(2)}) %copy-start.2) | copy-done | bytes 262168
  5.0 12.5 %shard_map.56.corr = f32[16,16,128]{2,1,0:T(8,128)S(1)} custom-call(bf16[4,32,1024]{2,1,0:T(8,128)(2,1)S(1)} %shard_map.55.folded, bf16[1024,1024]{1,0:T(8,128)(2,1)S(1)} %copy-done, bf16[1024,128]{1,0:T(8,128)(2,1)S(1)} %copy-done.2), custom_call_target="tpu_custom_call" | custom-call | tf_op jit(solution)/shard_map/pallas_call | solution.py:206
  17.5 0.0 copy-done.4
  17.5 1.3 %shard_map.57 = bf16[16,16,128]{2,1,0:T(8,128)(2,1)} custom-call(s32[1,16]{1,0:T(1,128)S(1)} %copy-done.4, f32[16,16,128]{2,1,0:T(8,128)S(1)} %shard_map.56.corr), custom_call_target="tpu_custom_call" | custom-call | tf_op jit(solution)/shard_map/pallas_call | solution.py:225
Async XLA Ops:
  0.0 1.0 %copy-start.1 = (bf16[4,36864]{1,0:T(4,128)(2,1)S(1)}, bf16[4,36864]{1,0:T(4,128)(2,1)}, u32[]{:S(2)}) copy-start(bf16[4,36864]{1,0:T(4,128)(2,1)} %traces.1) | copy-start | bytes 884740
  1.0 0.7 %copy-start.3 = (s32[8]{0:T(128)S(1)}, s32[8]{0:T(128)}, u32[]{:S(2)}) copy-start(s32[8]{0:T(128)} %offsets.1) | copy-start | bytes 100
  1.6 15.8 %copy-start.4 = (s32[1,16]{1,0:T(1,128)S(1)}, s32[1,16]{1,0:T(1,128)}, u32[]{:S(2)}) copy-start(s32[1,16]{1,0:T(1,128)} %slots.1) | copy-start | bytes 196
  2.4 1.6 %copy-start = (bf16[1024,1024]{1,0:T(8,128)(2,1)S(1)}, bf16[1024,1024]{1,0:T(8,128)(2,1)}, u32[]{:S(2)}) copy-start(bf16[1024,1024]{1,0:T(8,128)(2,1)} %constant.4.clone.dft) | copy-start | bytes 6291460
  4.0 0.9 %copy-start.2 = (bf16[1024,128]{1,0:T(8,128)(2,1)S(1)}, bf16[1024,128]{1,0:T(8,128)(2,1)}, u32[]{:S(2)}) copy-start(bf16[1024,128]{1,0:T(8,128)(2,1)} %constant.5.clone.lag) | copy-start | bytes 786436

commit v2 on v1

--- a/solution.py
+++ b/solution.py
@@ -23,7 +23,7 @@
     k = RADIX * np.arange(BINS)[None, :] + np.arange(RADIX)[:, None]
     t = np.arange(FOLD)[:, None, None]
     dft = 2.0 * math.pi / SEG_LEN * ((t * k[None]) % SEG_LEN)
-    dft = np.stack([np.cos(dft), -np.sin(dft)], axis=2).reshape(FOLD, 2 * NB)
+    dft = np.stack([np.cos(dft), -np.sin(dft)], axis=2).reshape(FOLD, RADIX, 2 * BINS).transpose(1, 0, 2)
     tau = LAG_STEP * (np.arange(LAGS) - LAGS // 2)
     lag = 2.0 * math.pi / SEG_LEN * ((k[:, :, None] * tau) % SEG_LEN)
     lag = np.stack([np.cos(lag), -np.sin(lag)], axis=1).reshape(2 * NB, LAGS)
@@ -34,7 +34,26 @@
     return jnp.dot(left, right, preferred_element_type=jnp.float32)
 
 
-def fold(segs, ch, offsets, traces, out, folded):
+def fold(segs, ch, offsets_in, slots_in, traces_in, out, pick, offsets, slots, traces, folded, chosen, in_sem):
+    moves = [
+        pltpu.make_async_copy(one, two, in_sem.at[i])
+        for i, (one, two) in enumerate([(offsets_in, offsets), (slots_in, slots), (traces_in, traces)])
+    ]
+    for move in moves:
+        move.start()
+    for move in moves[:2]:
+        move.wait()
+
+    n_cols = chosen.shape[1]
+    place = lax.broadcasted_iota(jnp.int32, (1, n_cols), 1)
+
+    def choose(q, _):
+        chosen[pl.ds(q, 1), :] = jnp.where(place == slots[0, q], 1.0, 0.0)
+        return 0
+
+    lax.fori_loop(0, n_cols, choose, 0)
+    pick[...] = chosen[...].astype(jnp.bfloat16)
+    moves[2].wait()
     window = traces.shape[1]
     lane = lax.broadcasted_iota(jnp.int32, (ch, 128), 1)
     for g in range(segs):
@@ -64,13 +83,27 @@
 
 def body(
     n_src, n_rcv, segs, ch,
-    folded, dft, lag, corr,
-    row_slots, col_slots, sources, receivers,
-    row_send, row_recv, col_send, col_recv,
+    folded_in, pick_in, dft_in, lag_in, placed,
+    folded, pick, dft, lag,
+    row_slots, col_slots, sources, receivers, corr,
+    in_sem, row_send, row_recv, col_send, col_recv,
 ):
     me_r = lax.axis_index("rcv")
     me_s = lax.axis_index("src")
     rows = segs * ch
+    near = me_s + 1 - 2 * lax.rem(me_s, 2)
+    across = n_src - 1 - me_s
+    far = lax.rem(me_s + 2, n_src)
+    inner = lax.rem(me_s, 3) != 0
+
+    moves = [
+        pltpu.make_async_copy(one, two, in_sem.at[i])
+        for i, (one, two) in enumerate(
+            [(folded_in, folded)] + [(dft_in.at[r], dft.at[r]) for r in range(RADIX)] + [(lag_in, lag), (pick_in, pick)]
+        )
+    ]
+    for move in moves:
+        move.start()
 
     barrier = pltpu.get_barrier_semaphore()
     for d in range(1, n_rcv):
@@ -83,11 +116,16 @@
     lax.fori_loop(1, n_src, greet, 0)
 
     width = 2 * BINS
-    p0 = dot(folded[0], dft[:, 0:width])
-    p2 = dot(folded[1], dft[:, 2 * width:3 * width])
+    moves[0].wait()
     both = folded[2:4].reshape(2 * rows, FOLD)
-    p1 = dot(both, dft[:, width:2 * width])
-    p3 = dot(both, dft[:, 3 * width:4 * width])
+    moves[1].wait()
+    p0 = dot(folded[0], dft[0])
+    moves[2].wait()
+    p1 = dot(both, dft[1])
+    moves[3].wait()
+    p2 = dot(folded[1], dft[2])
+    moves[4].wait()
+    p3 = dot(both, dft[3])
     parts = [
         p0[:, :BINS], p0[:, BINS:],
         p1[:rows, :BINS] + p1[rows:, BINS:], p1[:rows, BINS:] - p1[rows:, :BINS],
@@ -109,21 +147,35 @@
             device_id={"rcv": to}, device_id_type=MESH,
         )
 
-    def col_copy(to, slot):
+    def col_copy(to, slot, sem=None):
         return pltpu.make_async_remote_copy(
             src_ref=col_slots.at[slot], dst_ref=col_slots.at[slot],
-            send_sem=col_send.at[to], recv_sem=col_recv.at[slot],
+            send_sem=col_send.at[to if sem is None else sem], recv_sem=col_recv.at[slot],
             device_id={"src": to}, device_id_type=MESH,
         )
 
+    def send(d, _):
+        col_copy(lax.rem(me_s + d, n_src), me_s).start()
+        return 0
+
+    if n_src == 4:
+        col_copy(across, me_s).start()
+        col_copy(near, me_s).start()
+
+        @pl.when(jnp.logical_not(inner))
+        def _():
+            col_copy(far, me_s).start()
+    else:
+        lax.fori_loop(1, n_src, send, 0)
+
     for d in range(1, n_rcv):
         row_copy(lax.rem(me_r + d, n_rcv), me_r).start()
 
-    def send(d, _):
-        col_copy(lax.rem(me_s + d, n_src), me_s).start()
-        return 0
-
-    lax.fori_loop(1, n_src, send, 0)
+    if n_src == 4:
+        @pl.when(inner)
+        def _():
+            col_copy(across, across).wait_recv()
+            col_copy(near, across, far).start()
 
     for d in range(1, n_rcv):
         other = lax.rem(me_r + d, n_rcv)
@@ -151,8 +203,9 @@
                 im = im + (s_re * r_im - s_im * r_re)
             cross += [re.astype(jnp.bfloat16).reshape(ch * n_here, BINS), im.astype(jnp.bfloat16).reshape(ch * n_here, BINS)]
         done = dot(jnp.concatenate(cross, axis=1), lag[...]) * (1.0 / math.sqrt(segs * NB))
-        corr[pl.ds(p * ch, ch)] = done.reshape(ch, n_here, LAGS)
-
+        corr[pl.ds(pl.multiple_of(p * ch * n_here, ch * n_here), ch * n_here), :] = done
+
+    moves[5].wait()
     shard(me_s)
 
     def arrive(d, _):
@@ -161,7 +214,23 @@
         shard(other)
         return 0
 
-    lax.fori_loop(1, n_src, arrive, 0)
+    if n_src == 4:
+        col_copy(near, near).wait_recv()
+        shard(near)
+
+        @pl.when(jnp.logical_not(inner))
+        def _():
+            col_copy(across, across).wait_recv()
+
+        shard(across)
+        col_copy(far, far).wait_recv()
+        shard(far)
+    else:
+        lax.fori_loop(1, n_src, arrive, 0)
+
+    moves[6].wait()
+    for s in range(n_here):
+        placed[s] = dot(pick[...], corr[pl.ds(s, n_src * ch, stride=n_here), :].astype(jnp.bfloat16))
 
     for d in range(1, n_rcv):
         row_copy(lax.rem(me_r + d, n_rcv), me_r).wait_send()
@@ -171,19 +240,6 @@
         return 0
 
     lax.fori_loop(1, n_src, sent, 0)
-
-
-def arrange(slots, corr, out, placed):
-    n_cols, n_here = corr.shape[:2]
-
-    def place(q, _):
-        tile = corr[slots[0, q]]
-        for s in range(n_here):
-            placed[s, pl.ds(q, 1), :] = tile[s:s + 1]
-        return 0
-
-    lax.fori_loop(0, n_cols, place, 0)
-    out[...] = placed[...].astype(jnp.bfloat16)
 
 
 def on_device(n_src, n_rcv, traces, offsets, receiver_slots):
@@ -193,43 +249,48 @@
     rows = segs * ch
     n_here, n_cols = n_rcv * ch, n_src * ch
     vmem = pl.BlockSpec(memory_space=pltpu.VMEM)
-    smem = pl.BlockSpec(memory_space=pltpu.SMEM)
-    room = 40 * 1024 * 1024
-    folded = pl.pallas_call(
+    anywhere = pl.BlockSpec(memory_space=pl.ANY)
+    folded, pick = pl.pallas_call(
         functools.partial(fold, segs, ch),
-        out_shape=jax.ShapeDtypeStruct((RADIX, rows, FOLD), jnp.bfloat16),
-        in_specs=[smem, vmem],
-        out_specs=vmem,
-        scratch_shapes=[pltpu.VMEM((RADIX, rows, FOLD), jnp.float32)],
-        compiler_params=pltpu.CompilerParams(vmem_limit_bytes=room),
-    )(offsets, traces)
-    corr = pl.pallas_call(
+        out_shape=[
+            jax.ShapeDtypeStruct((RADIX, rows, FOLD), jnp.bfloat16),
+            jax.ShapeDtypeStruct((n_cols, n_cols), jnp.bfloat16),
+        ],
+        in_specs=[anywhere] * 3,
+        out_specs=[vmem] * 2,
+        scratch_shapes=[
+            pltpu.SMEM(offsets.shape, jnp.int32),
+            pltpu.SMEM(receiver_slots.shape, jnp.int32),
+            pltpu.VMEM(traces.shape, jnp.bfloat16),
+            pltpu.VMEM((RADIX, rows, FOLD), jnp.float32),
+            pltpu.VMEM((n_cols, n_cols), jnp.float32),
+            pltpu.SemaphoreType.DMA((3,)),
+        ],
+    )(offsets, receiver_slots, traces)
+    placed = pl.pallas_call(
         functools.partial(body, n_src, n_rcv, segs, ch),
-        out_shape=jax.ShapeDtypeStruct((n_cols, n_here, LAGS), jnp.float32),
-        in_specs=[vmem] * 3,
+        out_shape=jax.ShapeDtypeStruct((n_here, n_cols, LAGS), jnp.float32),
+        in_specs=[anywhere] * 4,
         out_specs=vmem,
         scratch_shapes=[
+            pltpu.VMEM((RADIX, rows, FOLD), jnp.bfloat16),
+            pltpu.VMEM((n_cols, n_cols), jnp.bfloat16),
+            pltpu.VMEM(dft.shape, jnp.bfloat16),
+            pltpu.VMEM(lag.shape, jnp.bfloat16),
             pltpu.VMEM((n_rcv, rows, 2 * NB), jnp.bfloat16),
             pltpu.VMEM((n_src, rows, 2 * NB), jnp.bfloat16),
             pltpu.VMEM((segs, n_here, 2 * NB), jnp.float32),
             pltpu.VMEM((rows, 2 * NB), jnp.float32),
+            pltpu.VMEM((n_here * n_cols, LAGS), jnp.float32),
+            pltpu.SemaphoreType.DMA((RADIX + 3,)),
             pltpu.SemaphoreType.DMA((n_rcv,)),
             pltpu.SemaphoreType.DMA((n_rcv,)),
             pltpu.SemaphoreType.DMA((n_src,)),
             pltpu.SemaphoreType.DMA((n_src,)),
         ],
-        compiler_params=pltpu.CompilerParams(
-            collective_id=0, has_side_effects=True, vmem_limit_bytes=room
-        ),
-    )(folded, jnp.asarray(dft), jnp.asarray(lag))
-    return pl.pallas_call(
-        arrange,
-        out_shape=jax.ShapeDtypeStruct((n_here, n_cols, LAGS), jnp.bfloat16),
-        in_specs=[smem, vmem],
-        out_specs=vmem,
-        scratch_shapes=[pltpu.VMEM((n_here, n_cols, LAGS), jnp.float32)],
-        compiler_params=pltpu.CompilerParams(vmem_limit_bytes=room),
-    )(receiver_slots, corr)
+        compiler_params=pltpu.CompilerParams(collective_id=0, has_side_effects=True),
+    )(folded, pick, jnp.asarray(dft), jnp.asarray(lag))
+    return placed.astype(jnp.bfloat16)
 
 
 def solution(mesh):

time: 19 us -> 17.7 us (0.932)
  local copies, waits for them, and re-layouts: 4.16 us -> 0 us
  other arithmetic: 0 us -> 1.54 us
  Pallas kernels: 14.6 us -> 16 us
    unnamed x10 -> x0, local copies, waits for them, and re-layouts: 4.16 us -> none
    pallas_call x1, Pallas kernels: 12.5 us -> 14.1 us  [on_device(): pl.pallas_call(functools.partial(body, n_src, n_rcv, segs, ch), out_shape...]
    convert_element_type x0 -> x1, other arithmetic: none -> 1.54 us  [on_device(): return placed.astype(jnp.bfloat16)]
    pallas_call x2 -> x1, Pallas kernels: 2.13 us -> 1.95 us  [on_device(): pl.pallas_call(functools.partial(fold, segs, ch), out_shape=[jax.ShapeDty...]
where the time goes in v2:
time: 17.7 us; the launch traced here: 17.6 us
  Pallas kernels  16 us (90%)
  other arithmetic  1.54 us (9%)
    pallas_call x1, Pallas kernels, on_device(): pl.pallas_call(functools.partial(body, n_src, n_rcv, segs, ch), out_shape...  14.1 us
    pallas_call x1, Pallas kernels, on_device(): pl.pallas_call(functools.partial(fold, segs, ch), out_shape=[jax.ShapeDty...  1.95 us
    convert_element_type x1, other arithmetic, on_device(): return placed.astype(jnp.bfloat16)  1.54 us

profile of v2, /device:TPU:0, one launch (start us, length us, event | category | flops | bytes accessed | tf_op | source)
XLA Modules:
  0.0 17.6 jit_solution(13797900887740051030)
XLA Ops:
  0.0 1.9 %shard_map.55 = (bf16[4,32,1024]{2,1,0:T(8,128)(2,1)}, bf16[16,16]{1,0:T(8,128)(2,1)}) custom-call(s32[8]{0:T(128)} %offsets_in.1, s32[1,16]{1,0:T(1,128)} %slots_in.1, bf16[4,36864]{1,0:T(4,128)(2,1)} %traces_in.1), custom_call_target="tpu_custom_call" | custom-call | tf_op jit(solution)/shard_map/pallas_call | solution.py:253
  2.0 14.1 %shard_map.56 = f32[16,16,128]{2,1,0:T(8,128)} custom-call(bf16[4,32,1024]{2,1,0:T(8,128)(2,1)} %get-tuple-element.7.folded_in, bf16[16,16]{1,0:T(8,128)(2,1)} %get-tuple-element.8.pick_in, bf16[4,1024,256]{2,1,0:T(8,128)(2,1)} %constant.4.clone.dft_in, bf16[1024,128]{1,0:T(8,128)(2,1)} %constant.5.clone.lag_in), custom_call_target="tpu_custom_call" | custom-call | tf_op jit(solution)/shard_map/pallas_call | solution.py:270
  16.0 1.5 %convert_element_type.3 = bf16[16,16,128]{2,1,0:T(8,128)(2,1)} convert(f32[16,16,128]{2,1,0:T(8,128)} %shard_map.56) | non-fusion elementwise | flops 32768 | bytes 196608 | tf_op jit(solution)/shard_map/convert_element_type | solution.py:293

commit v3 on v2

--- a/solution.py
+++ b/solution.py
@@ -27,17 +27,22 @@
     tau = LAG_STEP * (np.arange(LAGS) - LAGS // 2)
     lag = 2.0 * math.pi / SEG_LEN * ((k[:, :, None] * tau) % SEG_LEN)
     lag = np.stack([np.cos(lag), -np.sin(lag)], axis=1).reshape(2 * NB, LAGS)
-    return dft.astype(np.float32).astype(jnp.bfloat16), lag.astype(np.float32).astype(jnp.bfloat16)
+    dft = dft.reshape(RADIX * FOLD, 2 * BINS)
+    lag = lag.reshape(2, NB, LAGS).transpose(1, 0, 2).reshape(NB, 2 * LAGS)
+    return np.concatenate([dft, lag], axis=0).astype(np.float32).astype(jnp.bfloat16)
 
 
 def dot(left, right):
     return jnp.dot(left, right, preferred_element_type=jnp.float32)
 
 
-def fold(segs, ch, offsets_in, slots_in, traces_in, out, pick, offsets, slots, traces, folded, chosen, in_sem):
+def whiten(segs, ch, offsets_in, slots_in, traces_in, table, white, pick, offsets, slots, traces, dft, folded, chosen, in_sem):
     moves = [
         pltpu.make_async_copy(one, two, in_sem.at[i])
-        for i, (one, two) in enumerate([(offsets_in, offsets), (slots_in, slots), (traces_in, traces)])
+        for i, (one, two) in enumerate(
+            [(offsets_in, offsets), (slots_in, slots), (traces_in, traces)]
+            + [(table.at[r * FOLD:(r + 1) * FOLD], dft.at[r]) for r in range(RADIX)]
+        )
     ]
     for move in moves:
         move.start()
@@ -78,14 +83,31 @@
             folded[1, here, at] = even - odd
             folded[2, here, at] = x0 - x2
             folded[3, here, at] = x1 - x3
-    out[...] = folded[...].astype(jnp.bfloat16)
+    rows = segs * ch
+    both = folded[2:4].reshape(2 * rows, FOLD).astype(jnp.bfloat16)
+    moves[3].wait()
+    p0 = dot(folded[0].astype(jnp.bfloat16), dft[0])
+    moves[4].wait()
+    p1 = dot(both, dft[1])
+    moves[5].wait()
+    p2 = dot(folded[1].astype(jnp.bfloat16), dft[2])
+    moves[6].wait()
+    p3 = dot(both, dft[3])
+    parts = [
+        p0[:, :BINS], p0[:, BINS:],
+        p1[:rows, :BINS] + p1[rows:, BINS:], p1[:rows, BINS:] - p1[rows:, :BINS],
+        p2[:, :BINS], p2[:, BINS:],
+        p3[:rows, :BINS] - p3[rows:, BINS:], p3[:rows, BINS:] + p3[rows:, :BINS],
+    ]
+    spectra = jnp.concatenate(parts, axis=1)
+    energy = jnp.sum(spectra * spectra, axis=1, keepdims=True) * (1.0 / (2 * NB))
+    white[...] = (spectra * (1.0 / jnp.sqrt(energy + 1e-06))).astype(jnp.bfloat16)
 
 
 def body(
     n_src, n_rcv, segs, ch,
-    folded_in, pick_in, dft_in, lag_in, placed,
-    folded, pick, dft, lag,
-    row_slots, col_slots, sources, receivers, corr,
+    white, pick, table, out,
+    lag, row_slots, col_slots, sources, receivers, corr,
     in_sem, row_send, row_recv, col_send, col_recv,
 ):
     me_r = lax.axis_index("rcv")
@@ -99,7 +121,7 @@
     moves = [
         pltpu.make_async_copy(one, two, in_sem.at[i])
         for i, (one, two) in enumerate(
-            [(folded_in, folded)] + [(dft_in.at[r], dft.at[r]) for r in range(RADIX)] + [(lag_in, lag), (pick_in, pick)]
+            [(table.at[RADIX * FOLD:, h * LAGS:(h + 1) * LAGS], lag.at[h * NB:(h + 1) * NB]) for h in range(2)]
         )
     ]
     for move in moves:
@@ -115,29 +137,8 @@
 
     lax.fori_loop(1, n_src, greet, 0)
 
-    width = 2 * BINS
-    moves[0].wait()
-    both = folded[2:4].reshape(2 * rows, FOLD)
-    moves[1].wait()
-    p0 = dot(folded[0], dft[0])
-    moves[2].wait()
-    p1 = dot(both, dft[1])
-    moves[3].wait()
-    p2 = dot(folded[1], dft[2])
-    moves[4].wait()
-    p3 = dot(both, dft[3])
-    parts = [
-        p0[:, :BINS], p0[:, BINS:],
-        p1[:rows, :BINS] + p1[rows:, BINS:], p1[:rows, BINS:] - p1[rows:, :BINS],
-        p2[:, :BINS], p2[:, BINS:],
-        p3[:rows, :BINS] - p3[rows:, BINS:], p3[:rows, BINS:] + p3[rows:, :BINS],
-    ]
-    spectra = jnp.concatenate(parts, axis=1)
-    energy = jnp.sum(spectra * spectra, axis=1, keepdims=True) * (1.0 / (2 * NB))
-    white = (spectra * (1.0 / jnp.sqrt(energy + 1e-06))).astype(jnp.bfloat16)
-    row_slots[me_r] = white
-    col_slots[me_s] = white
-
+    row_slots[me_r] = white[...]
+    col_slots[me_s] = white[...]
     pl.semaphore_wait(barrier, n_rcv - 1 + n_src - 1)
 
     def row_copy(to, slot):
@@ -159,12 +160,11 @@
         return 0
 
     if n_src == 4:
-        col_copy(across, me_s).start()
+        @pl.when(inner)
+        def _():
+            col_copy(across, me_s).start()
+
         col_copy(near, me_s).start()
-
-        @pl.when(jnp.logical_not(inner))
-        def _():
-            col_copy(far, me_s).start()
     else:
         lax.fori_loop(1, n_src, send, 0)
 
@@ -176,6 +176,12 @@
         def _():
             col_copy(across, across).wait_recv()
             col_copy(near, across, far).start()
+
+        @pl.when(jnp.logical_not(inner))
+        def _():
+            col_copy(near, me_s).wait_send()
+            col_copy(across, me_s).start()
+            col_copy(far, me_s).start()
 
     for d in range(1, n_rcv):
         other = lax.rem(me_r + d, n_rcv)
@@ -186,6 +192,7 @@
             sources[g, j * ch:(j + 1) * ch, :] = block[g * ch:(g + 1) * ch]
 
     n_here = n_rcv * ch
+    width = 2 * BINS
 
     def shard(p):
         receivers[...] = col_slots[p].astype(jnp.float32)
@@ -205,7 +212,8 @@
         done = dot(jnp.concatenate(cross, axis=1), lag[...]) * (1.0 / math.sqrt(segs * NB))
         corr[pl.ds(pl.multiple_of(p * ch * n_here, ch * n_here), ch * n_here), :] = done
 
-    moves[5].wait()
+    for move in moves:
+        move.wait()
     shard(me_s)
 
     def arrive(d, _):
@@ -228,9 +236,8 @@
     else:
         lax.fori_loop(1, n_src, arrive, 0)
 
-    moves[6].wait()
     for s in range(n_here):
-        placed[s] = dot(pick[...], corr[pl.ds(s, n_src * ch, stride=n_here), :].astype(jnp.bfloat16))
+        out[s] = dot(pick[...], corr[pl.ds(s, n_src * ch, stride=n_here), :].astype(jnp.bfloat16)).astype(jnp.bfloat16)
 
     for d in range(1, n_rcv):
         row_copy(lax.rem(me_r + d, n_rcv), me_r).wait_send()
@@ -239,58 +246,67 @@
         col_copy(lax.rem(me_s + d, n_src), me_s).wait_send()
         return 0
 
-    lax.fori_loop(1, n_src, sent, 0)
+    if n_src == 4:
+        @pl.when(inner)
+        def _():
+            col_copy(near, me_s).wait_send()
+
+        col_copy(across, me_s).wait_send()
+        col_copy(far, me_s).wait_send()
+    else:
+        lax.fori_loop(1, n_src, sent, 0)
 
 
 def on_device(n_src, n_rcv, traces, offsets, receiver_slots):
-    dft, lag = tables()
+    table = jnp.asarray(tables())
     ch = traces.shape[0]
     segs = offsets.shape[0]
     rows = segs * ch
     n_here, n_cols = n_rcv * ch, n_src * ch
     vmem = pl.BlockSpec(memory_space=pltpu.VMEM)
-    anywhere = pl.BlockSpec(memory_space=pl.ANY)
-    folded, pick = pl.pallas_call(
-        functools.partial(fold, segs, ch),
+    hbm = pl.BlockSpec(memory_space=pltpu.HBM)
+    room = 40 * 1024 * 1024
+    white, pick = pl.pallas_call(
+        functools.partial(whiten, segs, ch),
         out_shape=[
-            jax.ShapeDtypeStruct((RADIX, rows, FOLD), jnp.bfloat16),
+            jax.ShapeDtypeStruct((rows, 2 * NB), jnp.bfloat16),
             jax.ShapeDtypeStruct((n_cols, n_cols), jnp.bfloat16),
         ],
-        in_specs=[anywhere] * 3,
+        in_specs=[hbm] * 4,
         out_specs=[vmem] * 2,
         scratch_shapes=[
             pltpu.SMEM(offsets.shape, jnp.int32),
             pltpu.SMEM(receiver_slots.shape, jnp.int32),
             pltpu.VMEM(traces.shape, jnp.bfloat16),
+            pltpu.VMEM((RADIX, FOLD, 2 * BINS), jnp.bfloat16),
             pltpu.VMEM((RADIX, rows, FOLD), jnp.float32),
             pltpu.VMEM((n_cols, n_cols), jnp.float32),
-            pltpu.SemaphoreType.DMA((3,)),
+            pltpu.SemaphoreType.DMA((RADIX + 3,)),
         ],
-    )(offsets, receiver_slots, traces)
-    placed = pl.pallas_call(
+        compiler_params=pltpu.CompilerParams(vmem_limit_bytes=room),
+    )(offsets, receiver_slots, traces, table)
+    return pl.pallas_call(
         functools.partial(body, n_src, n_rcv, segs, ch),
-        out_shape=jax.ShapeDtypeStruct((n_here, n_cols, LAGS), jnp.float32),
-        in_specs=[anywhere] * 4,
+        out_shape=jax.ShapeDtypeStruct((n_here, n_cols, LAGS), jnp.bfloat16),
+        in_specs=[vmem, vmem, hbm],
         out_specs=vmem,
         scratch_shapes=[
-            pltpu.VMEM((RADIX, rows, FOLD), jnp.bfloat16),
-            pltpu.VMEM((n_cols, n_cols), jnp.bfloat16),
-            pltpu.VMEM(dft.shape, jnp.bfloat16),
-            pltpu.VMEM(lag.shape, jnp.bfloat16),
+            pltpu.VMEM((2 * NB, LAGS), jnp.bfloat16),
             pltpu.VMEM((n_rcv, rows, 2 * NB), jnp.bfloat16),
             pltpu.VMEM((n_src, rows, 2 * NB), jnp.bfloat16),
             pltpu.VMEM((segs, n_here, 2 * NB), jnp.float32),
             pltpu.VMEM((rows, 2 * NB), jnp.float32),
             pltpu.VMEM((n_here * n_cols, LAGS), jnp.float32),
-            pltpu.SemaphoreType.DMA((RADIX + 3,)),
+            pltpu.SemaphoreType.DMA((2,)),
             pltpu.SemaphoreType.DMA((n_rcv,)),
             pltpu.SemaphoreType.DMA((n_rcv,)),
             pltpu.SemaphoreType.DMA((n_src,)),
             pltpu.SemaphoreType.DMA((n_src,)),
         ],
-        compiler_params=pltpu.CompilerParams(collective_id=0, has_side_effects=True),
-    )(folded, pick, jnp.asarray(dft), jnp.asarray(lag))
-    return placed.astype(jnp.bfloat16)
+        compiler_params=pltpu.CompilerParams(
+            collective_id=0, has_side_effects=True, vmem_limit_bytes=room
+        ),
+    )(white, pick, table)
 
 
 def solution(mesh):

time: 17.7 us -> 19.5 us (1.10)
  local copies, waits for them, and re-layouts: 0 us -> 4.57 us
  other arithmetic: 1.54 us -> 0 us
  Pallas kernels: 16 us -> 14.7 us
    unnamed x0 -> x11, local copies, waits for them, and re-layouts: none -> 4.57 us
    convert_element_type x1 -> x0, other arithmetic: 1.54 us -> none  [on_device(): return placed.astype(jnp.bfloat16)]
    pallas_call x1, Pallas kernels: 14.1 us -> 12.6 us  [on_device(): pl.pallas_call(functools.partial(body, n_src, n_rcv, segs, ch), out_shape...]
where the time goes in v3:
time: 19.5 us; the launch traced here: 19.3 us
  Pallas kernels  14.7 us (75%)
  local copies, waits for them, and re-layouts  4.57 us (23%)
    pallas_call x1, Pallas kernels, on_device(): pl.pallas_call(functools.partial(body, n_src, n_rcv, segs, ch), out_shape...  12.6 us
    unnamed x11, local copies, waits for them, and re-layouts  4.57 us
    pallas_call x1, Pallas kernels, on_device(): pl.pallas_call(functools.partial(whiten, segs, ch), out_shape=[jax.ShapeD...  2.12 us

profile of v3, /device:TPU:0, one launch (start us, length us, event | category | flops | bytes accessed | tf_op | source)
XLA Modules:
  0.0 19.3 jit_solution(3022924732587794555)
XLA Ops:
  0.0 0.0 copy-start
  0.0 1.7 %copy-done = bf16[4608,256]{1,0:T(8,128)(2,1)S(1)} copy-done((bf16[4608,256]{1,0:T(8,128)(2,1)S(1)}, bf16[4608,256]{1,0:T(8,128)(2,1)}, u32[]{:S(2)}) %copy-start) | copy-done | bytes 2359320
  1.7 0.0 copy-start.2
  1.7 1.0 %copy-done.2 = bf16[4,36864]{1,0:T(4,128)(2,1)S(1)} copy-done((bf16[4,36864]{1,0:T(4,128)(2,1)S(1)}, bf16[4,36864]{1,0:T(4,128)(2,1)}, u32[]{:S(2)}) %copy-start.2) | copy-done | bytes 294936
  2.6 0.0 copy-start.3
  2.6 0.7 %copy-done.3 = s32[8]{0:T(128)S(1)} copy-done((s32[8]{0:T(128)S(1)}, s32[8]{0:T(128)}, u32[]{:S(2)}) %copy-start.3) | copy-done | bytes 56
  3.3 0.0 copy-start.4
  3.3 0.7 %copy-done.4 = s32[1,16]{1,0:T(1,128)S(1)} copy-done((s32[1,16]{1,0:T(1,128)S(1)}, s32[1,16]{1,0:T(1,128)}, u32[]{:S(2)}) %copy-start.4) | copy-done | bytes 88
  3.9 0.0 copy-start.1
  3.9 2.1 %shard_map.46 = (bf16[32,1024]{1,0:T(8,128)(2,1)S(1)}, bf16[16,16]{1,0:T(8,128)(2,1)S(1)}) custom-call(s32[8]{0:T(128)S(1)} %copy-done.3, s32[1,16]{1,0:T(1,128)S(1)} %copy-done.4, bf16[4,36864]{1,0:T(4,128)(2,1)S(1)} %copy-done.2, bf16[4608,256]{1,0:T(8,128)(2,1)S(1)} %copy-done), custom_call_target="tpu_custom_call" | custom-call | tf_op jit(solution)/shard_map/pallas_call | solution.py:269
  6.1 0.0 copy-done.1
  6.1 12.6 %shard_map.47 = bf16[16,16,128]{2,1,0:T(8,128)(2,1)S(1)} custom-call(bf16[32,1024]{1,0:T(8,128)(2,1)S(1)} %get-tuple-element.7.white, bf16[16,16]{1,0:T(8,128)(2,1)S(1)} %get-tuple-element.8.pick, bf16[4608,256]{1,0:T(8,128)(2,1)S(1)} %copy-done.1), custom_call_target="tpu_custom_call" | custom-call | tf_op jit(solution)/shard_map/pallas_call | solution.py:288
  18.6 0.6 %copy.6 = bf16[16,16,128]{2,1,0:T(8,128)(2,1)} copy(bf16[16,16,128]{2,1,0:T(8,128)(2,1)S(1)} %shard_map.47) | data formatting | bytes 131072
Async XLA Ops:
  0.0 1.7 %copy-start = (bf16[4608,256]{1,0:T(8,128)(2,1)S(1)}, bf16[4608,256]{1,0:T(8,128)(2,1)}, u32[]{:S(2)}) copy-start(bf16[4608,256]{1,0:T(8,128)(2,1)} %constant.2.clone.table) | copy-start | bytes 7077892
  1.7 1.0 %copy-start.2 = (bf16[4,36864]{1,0:T(4,128)(2,1)S(1)}, bf16[4,36864]{1,0:T(4,128)(2,1)}, u32[]{:S(2)}) copy-start(bf16[4,36864]{1,0:T(4,128)(2,1)} %traces_in.1) | copy-start | bytes 884740
  2.6 0.7 %copy-start.3 = (s32[8]{0:T(128)S(1)}, s32[8]{0:T(128)}, u32[]{:S(2)}) copy-start(s32[8]{0:T(128)} %offsets_in.1) | copy-start | bytes 100
  3.3 0.7 %copy-start.4 = (s32[1,16]{1,0:T(1,128)S(1)}, s32[1,16]{1,0:T(1,128)}, u32[]{:S(2)}) copy-start(s32[1,16]{1,0:T(1,128)} %slots_in.1) | copy-start | bytes 196
  3.9 2.1 %copy-start.1 = (bf16[4608,256]{1,0:T(8,128)(2,1)S(1)}, bf16[4608,256]{1,0:T(8,128)(2,1)}, u32[]{:S(2)}) copy-start(bf16[4608,256]{1,0:T(8,128)(2,1)} %constant.2.clone.table) | copy-start | bytes 7077892

commit v4 on v3

--- a/solution.py
+++ b/solution.py
@@ -106,8 +106,8 @@
 
 def body(
     n_src, n_rcv, segs, ch,
-    white, pick, table, out,
-    lag, row_slots, col_slots, sources, receivers, corr,
+    white, pick_in, table, out,
+    pick, lag, row_slots, col_slots, sources, receivers, corr,
     in_sem, row_send, row_recv, col_send, col_recv,
 ):
     me_r = lax.axis_index("rcv")
@@ -116,12 +116,15 @@
     near = me_s + 1 - 2 * lax.rem(me_s, 2)
     across = n_src - 1 - me_s
     far = lax.rem(me_s + 2, n_src)
-    inner = lax.rem(me_s, 3) != 0
+    inner = (lax.rem(me_s, 3) + 1) // 2
+    second = far + inner * (across - far)
+    third = across + inner * (far - across)
 
     moves = [
         pltpu.make_async_copy(one, two, in_sem.at[i])
         for i, (one, two) in enumerate(
-            [(table.at[RADIX * FOLD:, h * LAGS:(h + 1) * LAGS], lag.at[h * NB:(h + 1) * NB]) for h in range(2)]
+            [(white, col_slots.at[me_s]), (white, row_slots.at[me_r]), (pick_in, pick)]
+            + [(table.at[RADIX * FOLD:, h * LAGS:(h + 1) * LAGS], lag.at[h * NB:(h + 1) * NB]) for h in range(2)]
         )
     ]
     for move in moves:
@@ -137,8 +140,8 @@
 
     lax.fori_loop(1, n_src, greet, 0)
 
-    row_slots[me_r] = white[...]
-    col_slots[me_s] = white[...]
+    moves[0].wait()
+    moves[1].wait()
     pl.semaphore_wait(barrier, n_rcv - 1 + n_src - 1)
 
     def row_copy(to, slot):
@@ -148,10 +151,10 @@
             device_id={"rcv": to}, device_id_type=MESH,
         )
 
-    def col_copy(to, slot, sem=None):
+    def col_copy(to, slot):
         return pltpu.make_async_remote_copy(
             src_ref=col_slots.at[slot], dst_ref=col_slots.at[slot],
-            send_sem=col_send.at[to if sem is None else sem], recv_sem=col_recv.at[slot],
+            send_sem=col_send.at[to], recv_sem=col_recv.at[slot],
             device_id={"src": to}, device_id_type=MESH,
         )
 
@@ -160,28 +163,13 @@
         return 0
 
     if n_src == 4:
-        @pl.when(inner)
-        def _():
-            col_copy(across, me_s).start()
-
-        col_copy(near, me_s).start()
+        for to in (across, far, near):
+            col_copy(to, me_s).start()
     else:
         lax.fori_loop(1, n_src, send, 0)
 
     for d in range(1, n_rcv):
         row_copy(lax.rem(me_r + d, n_rcv), me_r).start()
-
-    if n_src == 4:
-        @pl.when(inner)
-        def _():
-            col_copy(across, across).wait_recv()
-            col_copy(near, across, far).start()
-
-        @pl.when(jnp.logical_not(inner))
-        def _():
-            col_copy(near, me_s).wait_send()
-            col_copy(across, me_s).start()
-            col_copy(far, me_s).start()
 
     for d in range(1, n_rcv):
         other = lax.rem(me_r + d, n_rcv)
@@ -212,7 +200,7 @@
         done = dot(jnp.concatenate(cross, axis=1), lag[...]) * (1.0 / math.sqrt(segs * NB))
         corr[pl.ds(pl.multiple_of(p * ch * n_here, ch * n_here), ch * n_here), :] = done
 
-    for move in moves:
+    for move in moves[2:]:
         move.wait()
     shard(me_s)
 
@@ -223,16 +211,9 @@
         return 0
 
     if n_src == 4:
-        col_copy(near, near).wait_recv()
-        shard(near)
-
-        @pl.when(jnp.logical_not(inner))
-        def _():
-            col_copy(across, across).wait_recv()
-
-        shard(across)
-        col_copy(far, far).wait_recv()
-        shard(far)
+        for other in (near, second, third):
+            col_copy(other, other).wait_recv()
+            shard(other)
     else:
         lax.fori_loop(1, n_src, arrive, 0)
 
@@ -246,15 +227,7 @@
         col_copy(lax.rem(me_s + d, n_src), me_s).wait_send()
         return 0
 
-    if n_src == 4:
-        @pl.when(inner)
-        def _():
-            col_copy(near, me_s).wait_send()
-
-        col_copy(across, me_s).wait_send()
-        col_copy(far, me_s).wait_send()
-    else:
-        lax.fori_loop(1, n_src, sent, 0)
+    lax.fori_loop(1, n_src, sent, 0)
 
 
 def on_device(n_src, n_rcv, traces, offsets, receiver_slots):
@@ -264,15 +237,14 @@
     rows = segs * ch
     n_here, n_cols = n_rcv * ch, n_src * ch
     vmem = pl.BlockSpec(memory_space=pltpu.VMEM)
-    hbm = pl.BlockSpec(memory_space=pltpu.HBM)
-    room = 40 * 1024 * 1024
+    anywhere = pl.BlockSpec(memory_space=pl.ANY)
     white, pick = pl.pallas_call(
         functools.partial(whiten, segs, ch),
         out_shape=[
             jax.ShapeDtypeStruct((rows, 2 * NB), jnp.bfloat16),
             jax.ShapeDtypeStruct((n_cols, n_cols), jnp.bfloat16),
         ],
-        in_specs=[hbm] * 4,
+        in_specs=[anywhere] * 4,
         out_specs=[vmem] * 2,
         scratch_shapes=[
             pltpu.SMEM(offsets.shape, jnp.int32),
@@ -283,29 +255,27 @@
             pltpu.VMEM((n_cols, n_cols), jnp.float32),
             pltpu.SemaphoreType.DMA((RADIX + 3,)),
         ],
-        compiler_params=pltpu.CompilerParams(vmem_limit_bytes=room),
     )(offsets, receiver_slots, traces, table)
     return pl.pallas_call(
         functools.partial(body, n_src, n_rcv, segs, ch),
         out_shape=jax.ShapeDtypeStruct((n_here, n_cols, LAGS), jnp.bfloat16),
-        in_specs=[vmem, vmem, hbm],
+        in_specs=[anywhere] * 3,
         out_specs=vmem,
         scratch_shapes=[
+            pltpu.VMEM((n_cols, n_cols), jnp.bfloat16),
             pltpu.VMEM((2 * NB, LAGS), jnp.bfloat16),
             pltpu.VMEM((n_rcv, rows, 2 * NB), jnp.bfloat16),
             pltpu.VMEM((n_src, rows, 2 * NB), jnp.bfloat16),
             pltpu.VMEM((segs, n_here, 2 * NB), jnp.float32),
             pltpu.VMEM((rows, 2 * NB), jnp.float32),
             pltpu.VMEM((n_here * n_cols, LAGS), jnp.float32),
-            pltpu.SemaphoreType.DMA((2,)),
+            pltpu.SemaphoreType.DMA((5,)),
             pltpu.SemaphoreType.DMA((n_rcv,)),
             pltpu.SemaphoreType.DMA((n_rcv,)),
             pltpu.SemaphoreType.DMA((n_src,)),
             pltpu.SemaphoreType.DMA((n_src,)),
         ],
-        compiler_params=pltpu.CompilerParams(
-            collective_id=0, has_side_effects=True, vmem_limit_bytes=room
-        ),
+        compiler_params=pltpu.CompilerParams(collective_id=0, has_side_effects=True),
     )(white, pick, table)
 
 

time: 19.5 us -> 19 us (0.974)
  local copies, waits for them, and re-layouts: 4.57 us -> 1.47 us
  Pallas kernels: 14.7 us -> 17.3 us
    unnamed x11 -> x1, local copies, waits for them, and re-layouts: 4.57 us -> 1.47 us
    pallas_call x1, Pallas kernels: 12.6 us -> 14.2 us  [on_device(): pl.pallas_call(functools.partial(body, n_src, n_rcv, segs, ch), out_shape...]
    pallas_call x1, Pallas kernels: 2.12 us -> 3.06 us  [on_device(): pl.pallas_call(functools.partial(whiten, segs, ch), out_shape=[jax.ShapeD...]
where the time goes in v4:
time: 19 us; the launch traced here: 18.8 us
  Pallas kernels  17.3 us (91%)
  local copies, waits for them, and re-layouts  1.47 us (8%)
    pallas_call x1, Pallas kernels, on_device(): pl.pallas_call(functools.partial(body, n_src, n_rcv, segs, ch), out_shape...  14.2 us
    pallas_call x1, Pallas kernels, on_device(): pl.pallas_call(functools.partial(whiten, segs, ch), out_shape=[jax.ShapeD...  3.06 us
    unnamed x1, local copies, waits for them, and re-layouts  1.47 us

profile of v4, /device:TPU:0, one launch (start us, length us, event | category | flops | bytes accessed | tf_op | source)
XLA Modules:
  0.0 18.8 jit_solution(17826177707891578652)
XLA Ops:
  0.0 3.1 %shard_map.46 = (bf16[32,1024]{1,0:T(8,128)(2,1)}, bf16[16,16]{1,0:T(8,128)(2,1)}) custom-call(s32[8]{0:T(128)} %offsets_in.1, s32[1,16]{1,0:T(1,128)} %slots_in.1, bf16[4,36864]{1,0:T(4,128)(2,1)} %traces_in.1, bf16[4608,256]{1,0:T(8,128)(2,1)} %constant.2.clone.table), custom_call_target="tpu_custom_call" | custom-call | tf_op jit(solution)/shard_map/pallas_call | solution.py:241
  3.1 14.2 %shard_map.47 = bf16[16,16,128]{2,1,0:T(8,128)(2,1)} custom-call(bf16[32,1024]{1,0:T(8,128)(2,1)} %get-tuple-element.7.white, bf16[16,16]{1,0:T(8,128)(2,1)} %get-tuple-element.8.pick_in, bf16[4608,256]{1,0:T(8,128)(2,1)} %constant.2.clone.table), custom_call_target="tpu_custom_call" | custom-call | tf_op jit(solution)/shard_map/pallas_call | solution.py:259
  17.3 1.5 %copy.6 = bf16[16,16,128]{2,1,0:T(8,128)(2,1)} copy(bf16[16,16,128]{2,1,0:T(8,128)(2,1)} %shard_map.47) | data formatting | bytes 131072
